TPU v7x, 32 devices: a whole 2x2x4 slice. The times are simulated.
32 devices in a mesh: groups: 2 (over y), slab: 4 (over x, core), vol: 4 (over z).
Axes of the slice: x: 2, y: 2, z: 4, core: 2. Of those that a mesh axis runs over, the one named last changes fastest.
Arguments:
- density: float32 [16, 32, 256, 256], P(('groups', 'vol'), 'slab'), parts along dimension 0, may hold values from 0.1 to 10
- weights: float32 [16], P('groups'), parts along dimension 0, may hold values from 0.5 to 2
Outputs:
- barycenter: float32 [64, 256, 256], P(('groups', 'slab')), parts along dimension 0
- scaling: float32 [16, 32, 256, 256], P(('groups', 'vol'), 'slab'), parts along dimension 0
There are 2 independent parts, one for each index of `groups`. A program takes and returns all parts, laid end to end along the dimension named above; each array names one. Nothing has to cross between parts.
All inputs are finite; a program needn't handle non-finite values.
Results may differ from a plain program's by a relative error of at most 0.00002.
Values sent between devices are 32-bit elements; how exact they have to be, the bound alone decides.
A program may use at most 64 MiB of HBM per device.

v0:
```python
import jax
import jax.numpy as jnp
import numpy as np
from jax import lax
from jax.sharding import PartitionSpec as P

ITERS = 2


gauss_raw = np.exp(-0.5 * np.arange(-2, 3) ** 2)
kernel_taps = [float(entry) for entry in gauss_raw / gauss_raw.sum()]


def with_halo(block, sides, width):
    for axis, dim in sides:
        count = lax.axis_size(axis)
        forward = [(i, i + 1) for i in range(count - 1)]
        backward = [(target, source) for source, target in forward]
        low = lax.ppermute(
            lax.slice_in_dim(block, block.shape[dim] - width, None, axis=dim), axis, forward
        )
        high = lax.ppermute(lax.slice_in_dim(block, 0, width, axis=dim), axis, backward)
        block = jnp.concatenate([low, block, high], axis=dim)
    return block


def blur_valid(volume, along):
    length = volume.shape[along] - 4
    total = kernel_taps[0] * lax.slice_in_dim(volume, 0, length, axis=along)
    for offset in range(1, 5):
        total = total + kernel_taps[offset] * lax.slice_in_dim(
            volume, offset, offset + length, axis=along
        )
    return total


def blur_zero(volume, along):
    widths = [(0, 0)] * volume.ndim
    widths[along] = (2, 2)
    return blur_valid(jnp.pad(volume, widths), along)


def heat_padded(padded):
    return blur_zero(blur_zero(blur_valid(padded, 1), 2), 3)


def per_device(density, weights):
    own_count = density.shape[0]
    norm_weights = weights / jnp.sum(weights)
    start = lax.axis_index("vol") * own_count
    own_weights = lax.dynamic_slice_in_dim(norm_weights, start, own_count)
    scaling = jnp.ones_like(density)
    center = jnp.zeros(density.shape[1:], jnp.float32)
    for sweep in range(ITERS):
        padded = with_halo(scaling, (("slab", 1),), 2)
        quotient = density / heat_padded(padded)
        padded_quotient = with_halo(quotient, (("slab", 1),), 2)
        spread = heat_padded(padded_quotient)
        marginal = scaling * spread
        partial_value = jnp.sum(own_weights[:, None, None, None] * jnp.log(marginal), axis=0)
        log_mean = lax.psum(partial_value, "vol")
        center = jnp.exp(log_mean)
        scaling = scaling * center[None] / marginal
    return (center, scaling)


def solution(mesh):
    in_specs = (P(("groups", "vol"), "slab", None, None), P("groups"))
    out_specs = (P(("groups", "slab"), None, None), P(("groups", "vol"), "slab", None, None))
    return jax.shard_map(
        per_device, mesh=mesh, in_specs=in_specs, out_specs=out_specs, check_vma=False
    )
```

profile of v0, /device:TPU:0, one launch (start us, length us, event | category | flops | bytes accessed | tf_op | source)
XLA Modules:
  0.0 341.2 jit_solution(1984813387054107911)
XLA Ops:
  7.2 0.0 all-reduce.13.cloned.1.call-start
  7.2 0.1 broadcast.35
  7.3 1.3 collective-permute-start.1
  8.6 3.1 collective-permute-start
  11.7 0.1 collective-permute-done.1
  11.8 2.1 collective-permute-done
  13.9 0.6 fusion.28
  14.5 0.0 copy-start.3
  14.5 2.3 multiply_add_fusion.3
  16.9 0.0 copy-done.3
  16.9 4.7 %fusion.37 = f32[2,8,256,256]{3,2,1,0:T(8,128)S(1)} fusion(f32[2,8,256,256]{3,2,1,0:T(8,128)S(1)} %copy-done.3, f32[2,8,256,256]{3,2,1,0:T(8,128)S(1)} %multiply_add_fusion.3), kind=kLoop, calls=%fused_computation.69 | loop fusion | flops 10485760 | bytes 12582912 | tf_op jit(solution)/shard_map/div | solution.py:56
  21.6 0.0 copy-start.2
  21.6 2.0 copy-done.2
  23.6 0.0 copy-start.6
  23.6 1.2 fusion.81
  24.8 14.0 %collective-permute-start.2 = (f32[2,2,256,256]{3,2,1,0:T(8,128)}, f32[2,2,256,256]{3,2,1,0:T(8,128)S(1)}, u32[]{:S(2)}, u32[]{:S(2)}) collective-permute-start(f32[2,2,256,256]{3,2,1,0:T(8,128)} %get-tuple-element.10), channel_id=1, source_target_pairs={{0,4},{4,8},{8,12},{1,5},{5,9},{9,13},{2,6},{6,10},{10,14},{3,7},{... | collective-permute-start | bytes 3145736 | tf_op jit(solution)/shard_map/ppermute | solution.py:19
  38.7 1.3 collective-permute-start.3
  40.1 0.0 copy-done.6
  40.1 0.7 reduce_sum.27
  40.7 0.6 broadcast_divide_fusion.1
  41.4 0.1 dynamic_slice.3
  41.4 0.0 collective-permute-done.2
  41.4 3.8 %collective-permute-done.3 = f32[2,2,256,256]{3,2,1,0:T(8,128)S(1)} collective-permute-done((f32[2,2,256,256]{3,2,1,0:T(8,128)S(1)}, f32[2,2,256,256]{3,2,1,0:T(8,128)S(1)}, u32[]{:S(2)}, u32[]{:S(2)}) %collective-permute-start.3) | collective-permute-done | bytes 1048608 | tf_op jit(solution)/shard_map/ppermute | solution.py:22
  45.2 8.0 %fusion.19 = f32[2,8,256,256]{3,2,1,0:T(8,128)S(1)} fusion(f32[2,8,256,256]{3,2,1,0:T(8,128)} %copy-done.2, f32[2,2,256,256]{3,2,1,0:T(8,128)S(1)} %collective-permute-done.3, f32[2,2,256,256]{3,2,1,0:T(8,128)S(1)} %collective-permute-done.2), kind=kLoop, calls=%fused_computation.51 | loop fusion | flops 13631488 | bytes 10485760 | tf_op jit(solution)/shard_map/add | solution.py:31
  53.3 2.3 multiply_add_fusion.2
  55.6 7.4 %multiply_reduce_fusion.1 = (f32[8,256,256]{2,1,0:T(8,128)}, f32[2,8,256,256]{3,2,1,0:T(8,128)}) fusion(f32[2]{0:T(128)S(1)} %dynamic_slice.3, f32[2,8,256,256]{3,2,1,0:T(8,128)S(1)} %multiply_add_fusion.2), kind=kLoop, calls=%fused_computation.119 | loop fusion | flops 11010048 | bytes 10485768 | tf_op jit(solution)/shard_map/reduce_sum | solution.py:60
  63.0 0.0 all-reduce.13.cloned.1.call-update
  63.0 0.0 all-reduce.15.cloned.1.call-start
  63.0 98.6 %all-reduce.13.cloned.1.call-done = f32[8,256,256]{2,1,0:T(8,128)} async-done(((f32[8,256,256]{2,1,0:T(8,128)}), f32[8,256,256]{2,1,0:T(8,128)}) %all-reduce.13.cloned.1.call-update) | async-done | bytes 2097168 | tf_op jit(solution)/shard_map/psum | solution.py:61
  161.7 0.0 copy-start
  161.7 2.0 exp.6
  163.7 0.8 copy-done
  164.5 0.5 broadcast_divide_fusion
  165.1 0.1 fusion.80
  165.2 1.8 collective-permute-start.4
  167.0 1.5 collective-permute-start.5
  168.5 0.7 collective-permute-done.4
  169.2 3.5 %collective-permute-done.5 = f32[2,2,256,256]{3,2,1,0:T(8,128)S(1)} collective-permute-done((f32[2,2,256,256]{3,2,1,0:T(8,128)S(1)}, f32[2,2,256,256]{3,2,1,0:T(8,128)S(1)}, u32[]{:S(2)}, u32[]{:S(2)}) %collective-permute-start.5) | collective-permute-done | bytes 1048608 | tf_op jit(solution)/shard_map/ppermute | solution.py:22
  172.8 2.9 fusion.11
  175.6 0.0 copy-start.4
  175.6 11.3 %multiply_add_fusion.1 = f32[2,8,256,256]{3,2,1,0:T(8,128)} fusion(f32[2,8,256,256]{3,2,1,0:T(8,128)} %fusion.11), kind=kLoop, calls=%fused_computation.116 | loop fusion | flops 9437184 | bytes 8388608 | tf_op jit(solution)/shard_map/add | solution.py:31
  186.9 0.0 copy-done.4
  186.9 12.3 %fusion.54 = f32[2,8,256,256]{3,2,1,0:T(8,128)S(1)} fusion(f32[2,8,256,256]{3,2,1,0:T(8,128)S(1)} %copy-done.4, f32[2,8,256,256]{3,2,1,0:T(8,128)} %multiply_add_fusion.1), kind=kLoop, calls=%fused_computation.86 | loop fusion | flops 10485760 | bytes 12582912 | tf_op jit(solution)/shard_map/div | solution.py:56
  199.2 0.1 fusion.79
  199.4 14.0 %collective-permute-start.6 = (f32[2,2,256,256]{3,2,1,0:T(8,128)S(1)}, f32[2,2,256,256]{3,2,1,0:T(8,128)S(1)}, u32[]{:S(2)}, u32[]{:S(2)}) collective-permute-start(f32[2,2,256,256]{3,2,1,0:T(8,128)S(1)} %get-tuple-element.6), channel_id=1, source_target_pairs={{0,4},{4,8},{8,12},{1,5},{5,9},{9,13},{2,6},{6,10},{10,14},{3,7},{... | collective-permute-start | bytes 3145736 | tf_op jit(solution)/shard_map/ppermute | solution.py:19
  213.4 1.3 collective-permute-start.7
  214.7 0.9 collective-permute-done.6
  215.6 2.4 collective-permute-done.7
  218.0 2.3 fusion.3
  220.3 2.3 multiply_add_fusion
  222.6 7.5 %multiply_reduce_fusion = (f32[8,256,256]{2,1,0:T(8,128)}, f32[2,8,256,256]{3,2,1,0:T(8,128)}) fusion(f32[2]{0:T(128)S(1)} %dynamic_slice.3, f32[2,8,256,256]{3,2,1,0:T(8,128)S(1)} %multiply_add_fusion, f32[2,8,256,256]{3,2,1,0:T(8,128)S(1)} %copy-done, f32[8,256,256]{2,1,0:T(8,128)S(1)} %exp.6), kind=kLoop, calls=%fused_computation.112 | loop fusion | flops 13107200 | bytes 16777224 | tf_op jit(solution)/shard_map/reduce_sum | solution.py:60
  230.1 0.0 all-reduce.15.cloned.1.call-update
  230.2 95.9 %all-reduce.15.cloned.1.call-done = f32[8,256,256]{2,1,0:T(8,128)} async-done(((f32[8,256,256]{2,1,0:T(8,128)}), f32[8,256,256]{2,1,0:T(8,128)}) %all-reduce.15.cloned.1.call-update) | async-done | bytes 2097168 | tf_op jit(solution)/shard_map/psum | solution.py:61
  326.0 0.0 copy-start.1
  326.1 2.0 exp.7
  328.1 0.0 copy-start.5
  328.1 0.8 copy-done.1
  328.9 5.5 %multiply_divide_fusion = f32[2,8,256,256]{3,2,1,0:T(8,128)} fusion(f32[2,8,256,256]{3,2,1,0:T(8,128)} %get-tuple-element.3, f32[8,256,256]{2,1,0:T(8,128)S(1)} %exp.7, f32[2,8,256,256]{3,2,1,0:T(8,128)S(1)} %copy-done.1, f32[8,256,256]{2,1,0:T(8,128)S(1)} %exp.6), kind=kLoop, calls=%fused_computation.111 | loop fusion | flops 3145728 | bytes 16777216 | tf_op jit(solution)/shard_map/div | solution.py:63
  334.4 0.0 copy-done.5
Async XLA Ops:
  7.2 154.5 %all-reduce.13.cloned.1.call-start = ((), (), s32[]{:S(2)}) async-start(), calls=%async_computation | async-start | bytes 4194304 | tf_op jit(solution)/shard_map/psum | solution.py:61
  7.3 4.6 %collective-permute-start.1 = (f32[2,2,256,256]{3,2,1,0:T(8,128)S(1)}, f32[2,2,256,256]{3,2,1,0:T(8,128)S(1)}, u32[]{:S(2)}, u32[]{:S(2)}) collective-permute-start(f32[2,2,256,256]{3,2,1,0:T(8,128)S(1)} %broadcast.35), channel_id=1, source_target_pairs={{4,0},{8,4},{12,8},{5,1},{9,5},{13,9},{6,2},{10,6},{14,10},{7,3},{... | collective-permute-start | bytes 3145736 | tf_op jit(solution)/shard_map/ppermute | solution.py:22
  8.6 5.3 %collective-permute-start = (f32[2,2,256,256]{3,2,1,0:T(8,128)S(1)}, f32[2,2,256,256]{3,2,1,0:T(8,128)S(1)}, u32[]{:S(2)}, u32[]{:S(2)}) collective-permute-start(f32[2,2,256,256]{3,2,1,0:T(8,128)S(1)} %broadcast.35), channel_id=1, source_target_pairs={{0,4},{4,8},{8,12},{1,5},{5,9},{9,13},{2,6},{6,10},{10,14},{3,7},{... | collective-permute-start | bytes 3145736 | tf_op jit(solution)/shard_map/ppermute | solution.py:19
  14.5 2.4 copy-start.3
  21.6 2.0 copy-start.2
  23.6 16.5 %copy-start.6 = (f32[8]{0:T(128)S(1)}, f32[8]{0:T(128)}, u32[]{:S(2)}) copy-start(f32[8]{0:T(128)} %param.3) | copy-start | bytes 100
  24.8 16.7 %collective-permute-start.2 = (f32[2,2,256,256]{3,2,1,0:T(8,128)}, f32[2,2,256,256]{3,2,1,0:T(8,128)S(1)}, u32[]{:S(2)}, u32[]{:S(2)}) collective-permute-start(f32[2,2,256,256]{3,2,1,0:T(8,128)} %get-tuple-element.10), channel_id=1, source_target_pairs={{0,4},{4,8},{8,12},{1,5},{5,9},{9,13},{2,6},{6,10},{10,14},{3,7},{... | collective-permute-start | bytes 3145736 | tf_op jit(solution)/shard_map/ppermute | solution.py:19
  38.7 6.5 %collective-permute-start.3 = (f32[2,2,256,256]{3,2,1,0:T(8,128)S(1)}, f32[2,2,256,256]{3,2,1,0:T(8,128)S(1)}, u32[]{:S(2)}, u32[]{:S(2)}) collective-permute-start(f32[2,2,256,256]{3,2,1,0:T(8,128)S(1)} %get-tuple-element.11), channel_id=1, source_target_pairs={{4,0},{8,4},{12,8},{5,1},{9,5},{13,9},{6,2},{10,6},{14,10},{7,3},{... | collective-permute-start | bytes 3145736 | tf_op jit(solution)/shard_map/ppermute | solution.py:22
  63.0 263.0 %all-reduce.15.cloned.1.call-start = ((), (), s32[]{:S(2)}) async-start(), calls=%async_computation.1 | async-start | bytes 4194304 | tf_op jit(solution)/shard_map/psum | solution.py:61
  161.7 2.8 copy-start
  165.2 4.0 %collective-permute-start.4 = (f32[2,2,256,256]{3,2,1,0:T(8,128)S(1)}, f32[2,2,256,256]{3,2,1,0:T(8,128)S(1)}, u32[]{:S(2)}, u32[]{:S(2)}) collective-permute-start(f32[2,2,256,256]{3,2,1,0:T(8,128)S(1)} %get-tuple-element.8), channel_id=1, source_target_pairs={{0,4},{4,8},{8,12},{1,5},{5,9},{9,13},{2,6},{6,10},{10,14},{3,7},{... | collective-permute-start | bytes 3145736 | tf_op jit(solution)/shard_map/ppermute | solution.py:19
  167.0 5.7 %collective-permute-start.5 = (f32[2,2,256,256]{3,2,1,0:T(8,128)S(1)}, f32[2,2,256,256]{3,2,1,0:T(8,128)S(1)}, u32[]{:S(2)}, u32[]{:S(2)}) collective-permute-start(f32[2,2,256,256]{3,2,1,0:T(8,128)S(1)} %get-tuple-element.9), channel_id=1, source_target_pairs={{4,0},{8,4},{12,8},{5,1},{9,5},{13,9},{6,2},{10,6},{14,10},{7,3},{... | collective-permute-start | bytes 3145736 | tf_op jit(solution)/shard_map/ppermute | solution.py:22
  175.6 11.3 %copy-start.4 = (f32[2,8,256,256]{3,2,1,0:T(8,128)S(1)}, f32[2,8,256,256]{3,2,1,0:T(8,128)}, u32[]{:S(2)}) copy-start(f32[2,8,256,256]{3,2,1,0:T(8,128)} %param.2) | copy-start | bytes 12582916
  199.4 16.2 %collective-permute-start.6 = (f32[2,2,256,256]{3,2,1,0:T(8,128)S(1)}, f32[2,2,256,256]{3,2,1,0:T(8,128)S(1)}, u32[]{:S(2)}, u32[]{:S(2)}) collective-permute-start(f32[2,2,256,256]{3,2,1,0:T(8,128)S(1)} %get-tuple-element.6), channel_id=1, source_target_pairs={{0,4},{4,8},{8,12},{1,5},{5,9},{9,13},{2,6},{6,10},{10,14},{3,7},{... | collective-permute-start | bytes 3145736 | tf_op jit(solution)/shard_map/ppermute | solution.py:19
  213.4 4.6 %collective-permute-start.7 = (f32[2,2,256,256]{3,2,1,0:T(8,128)S(1)}, f32[2,2,256,256]{3,2,1,0:T(8,128)S(1)}, u32[]{:S(2)}, u32[]{:S(2)}) collective-permute-start(f32[2,2,256,256]{3,2,1,0:T(8,128)S(1)} %get-tuple-element.7), channel_id=1, source_target_pairs={{4,0},{8,4},{12,8},{5,1},{9,5},{13,9},{6,2},{10,6},{14,10},{7,3},{... | collective-permute-start | bytes 3145736 | tf_op jit(solution)/shard_map/ppermute | solution.py:22
  326.0 2.8 copy-start.1
  328.1 6.3 %copy-start.5 = (f32[8,256,256]{2,1,0:T(8,128)}, f32[8,256,256]{2,1,0:T(8,128)S(1)}, u32[]{:S(2)}) copy-start(f32[8,256,256]{2,1,0:T(8,128)S(1)} %exp.7) | copy-start | bytes 6291460
Sparse Core Ops, SparseCore 0:
  63.1 98.5 all-reduce.12
  230.3 95.7 all-reduce.14
where the time goes:
time: 342 us; the launch traced here: 341 us
  waiting for transfers between devices  208 us (61%)
  other arithmetic  71.3 us (21%)
  starting transfers between devices  38.3 us (11%)
  between operations  14.3 us (4%)
  local copies, waits for them, and re-layouts  9.25 us (3%)
    psum x2, waiting for transfers between devices, per_device(): log_mean = lax.psum(partial_value, 'vol')  195 us
    ppermute x4, starting transfers between devices, with_halo(): lax.ppermute(lax.slice_in_dim(block, block.shape[dim] - width, None, axis...  32.9 us
    add x8, other arithmetic, blur_valid(): total + kernel_taps[offset] * lax.slice_in_dim(volume, offset, offset + l...  32.2 us
    div x2, other arithmetic, per_device(): quotient = density / heat_padded(padded)  17 us
    reduce_sum x2, other arithmetic, per_device(): jnp.sum(own_weights[:, None, None, None] * jnp.log(marginal), axis=0)  14.8 us
    ppermute x4, waiting for transfers between devices, with_halo(): lax.ppermute(lax.slice_in_dim(block, 0, width, axis=dim), axis, backward)  9.82 us
  transfers between devices with their start and end apart: 10, of which 9 were waited for; matrix products, arithmetic and copies ran while one was open for 0% of the time, Pallas kernels for 0%

commit v1 on v0

v1 whole, which is shorter than its diff:
```python
import functools

import jax
import jax.numpy as jnp
import numpy as np
from jax import lax
from jax.experimental import pallas as pl
from jax.experimental.pallas import tpu as pltpu
from jax.sharding import PartitionSpec as P

ITERS = 2
HALO = 2
CHUNKS = 4

gauss_raw = np.exp(-0.5 * np.arange(-2, 3) ** 2)
kernel_taps = [float(entry) for entry in gauss_raw / gauss_raw.sum()]
edge_sums = [sum(kernel_taps[2:]), sum(kernel_taps[1:]), sum(kernel_taps)]


def per_distance(distance):
    inverse = [1.0 / entry for entry in edge_sums]
    inner = jnp.where(distance == 1, inverse[1], inverse[2])
    return jnp.where(distance == 0, inverse[0], inner).astype(jnp.float32)


def band(size):
    rows = lax.broadcasted_iota(jnp.int32, (size, size), 0)
    gap = jnp.abs(rows - lax.broadcasted_iota(jnp.int32, (size, size), 1))
    inner = jnp.where(gap == 1, kernel_taps[1], jnp.where(gap == 2, kernel_taps[0], 0.0))
    return jnp.where(gap == 0, kernel_taps[2], inner).astype(jnp.float32)


def kernel(
    slabs, vols,
    weights, density, center_out, scaling_out,
    dens, scal, quot, marg, cent, acc, outer, inner, inverse, band_x, band_y,
    local_sem, out_sem, d_send, d_recv, s_send, s_recv, q_send, q_recv,
    up_send, down_send, outer_recv, inner_recv,
):
    own, nz, nx, ny = density.shape
    total_nz = nz * slabs
    rows = nx // CHUNKS
    steps = nz * CHUNKS
    slab, vol = lax.axis_index("slab"), lax.axis_index("vol")
    half = vols // 2
    low_side = vol < half
    inward = jnp.where(low_side, vol + 1, vol - 1)
    outward = jnp.where(low_side, vol - 1, vol + 1)
    depth = jnp.where(low_side, half - 1 - vol, vol - half)
    is_center = depth == 0
    has_outer = depth < half - 1
    lag = 2 + 5 * depth
    has_low, has_high = slab > 0, slab < slabs - 1

    barrier = pltpu.get_barrier_semaphore()

    def greet(device):
        pl.semaphore_signal(barrier, inc=1, device_id=device, device_id_type=pl.DeviceIdType.MESH)

    pl.when(has_low)(lambda: greet({"slab": slab - 1}))
    pl.when(has_high)(lambda: greet({"slab": slab + 1}))
    greet({"vol": inward})
    pl.when(has_outer)(lambda: greet({"vol": outward}))

    loads = [
        pltpu.make_async_copy(density.at[k], dens.at[k, pl.ds(HALO, nz)], local_sem.at[k])
        for k in range(own)
    ]
    for load in loads:
        load.start()

    def remote(src, dst, send, recv, device):
        return pltpu.make_async_remote_copy(
            src_ref=src, dst_ref=dst, send_sem=send, recv_sem=recv,
            device_id=device, device_id_type=pl.DeviceIdType.MESH,
        )

    def density_low(k):
        return remote(
            density.at[k, pl.ds(0, HALO)], dens.at[k, pl.ds(nz + HALO, HALO)],
            d_send.at[0, k], d_recv.at[0, k], {"slab": slab - 1},
        )

    def density_high(k):
        return remote(
            density.at[k, pl.ds(nz - HALO, HALO)], dens.at[k, pl.ds(0, HALO)],
            d_send.at[1, k], d_recv.at[1, k], {"slab": slab + 1},
        )

    def plane_low(buf, send, recv, k, p):
        return remote(
            buf.at[k, p + HALO], buf.at[k, p + HALO + nz],
            send.at[0, k, p], recv.at[0, k, p], {"slab": slab - 1},
        )

    def plane_high(buf, send, recv, k, p):
        at = p - (nz - HALO)
        return remote(
            buf.at[k, p + HALO], buf.at[k, at],
            send.at[1, k, at], recv.at[1, k, at], {"slab": slab + 1},
        )

    waits = jnp.where(has_low, 1, 0) + jnp.where(has_high, 1, 0) + jnp.where(has_outer, 2, 1)
    pl.semaphore_wait(barrier, waits)

    @pl.when(has_low)
    def _():
        for k in range(own):
            density_low(k).start()

    @pl.when(has_high)
    def _():
        for k in range(own):
            density_high(k).start()

    @pl.when(jnp.logical_not(has_low))
    def _():
        for buf in (dens, scal, quot):
            buf[:, 0:HALO] = jnp.zeros((own, HALO, nx, ny), jnp.float32)

    @pl.when(jnp.logical_not(has_high))
    def _():
        for buf in (dens, scal, quot):
            buf[:, nz + HALO :] = jnp.zeros((own, HALO, nx, ny), jnp.float32)

    band_x[...] = band(nx)
    band_y[...] = band(ny)
    at_x = lax.broadcasted_iota(jnp.int32, (nx, ny), 0)
    at_y = lax.broadcasted_iota(jnp.int32, (nx, ny), 1)
    inverse[...] = per_distance(jnp.minimum(at_x, nx - 1 - at_x)) * per_distance(
        jnp.minimum(at_y, ny - 1 - at_y)
    )

    count = weights.shape[0]
    weight_sum = weights[0]
    for k in range(1, count):
        weight_sum = weight_sum + weights[k]
    norm = [
        jnp.full((1, ny), weights[vol * own + k], jnp.float32)
        / jnp.full((1, ny), weight_sum, jnp.float32)
        for k in range(own)
    ]

    def in_plane(value):
        dot = functools.partial(
            jnp.dot, precision=lax.Precision.HIGHEST, preferred_element_type=jnp.float32
        )
        return dot(band_x[...], dot(value, band_y[...]))

    def along_z(buf, k, p):
        total = kernel_taps[0] * (buf[k, p] + buf[k, p + 4])
        total = total + kernel_taps[1] * (buf[k, p + 1] + buf[k, p + 3])
        return total + kernel_taps[2] * buf[k, p + 2]

    def faces(i):
        return i // 2 + (i % 2) * (nz - 1 - 2 * (i // 2))

    def order_first(i):
        late, last = (i + nz - 2) // nz, (i + nz - 6) // nz
        return (1 - late) * (i + 2) + (late - last) * faces(jnp.maximum(i - 2, 0)) + last * (i - 2)

    def order_faces(i):
        late = (i + nz - 4) // nz
        return (1 - late) * faces(i) + late * (i - 2)

    def order_second(i):
        late = (i + 4) // nz
        return (1 - late) * (i + 2) + late * faces(jnp.maximum(i - (nz - 4), 0))

    def up_center(t, g):
        return remote(
            acc.at[t, g], inner.at[t, g], up_send.at[t, g], inner_recv.at[t, g], {"vol": inward}
        )

    def up_other(t, g):
        return remote(
            acc.at[t, g], outer.at[t, g], up_send.at[t, g], outer_recv.at[t, g], {"vol": inward}
        )

    def down_copy(t, g):
        return remote(
            inner.at[t, g], inner.at[t, g], down_send.at[t, g], inner_recv.at[t, g],
            {"vol": outward},
        )

    def up(t, g):
        @pl.when(has_outer)
        def _():
            up_other(t, g).wait_recv()
            acc[t, g] = acc[t, g] + outer[t, g]

        pl.when(is_center)(lambda: up_center(t, g).start())
        pl.when(jnp.logical_not(is_center))(lambda: up_other(t, g).start())

    def down(t, g, use):
        down_copy(t, g).wait_recv()

        @pl.when(is_center)
        def _():
            inner[t, g] = inner[t, g] + acc[t, g]

        pl.when(has_outer)(lambda: down_copy(t, g).start())
        use(g)

    def all_reduce(t, order, compute, use):
        def step(i, _):
            part = compute(i, order(i))
            for c in range(CHUNKS):
                acc[t, i * CHUNKS + c] = part[c * rows : (c + 1) * rows]

            def chunk(c, _):
                g = i * CHUNKS + c
                up(t, g)
                pl.when(g >= lag)(lambda: down(t, g - lag, use))
                return 0

            lax.fori_loop(0, CHUNKS, chunk, 0)
            return 0

        lax.fori_loop(0, nz, step, 0)

        def tail(g, _):
            down(t, g, use)
            return 0

        lax.fori_loop(steps - lag, steps, tail, 0)

    def weighted(k, value):
        return norm[k] * jnp.log(value)

    for load in loads:
        load.wait()

    def first_compute(i, p):
        @pl.when(i == 2)
        def _():
            @pl.when(has_low)
            def _():
                for k in range(own):
                    density_high(k).wait_recv()

            @pl.when(has_high)
            def _():
                for k in range(own):
                    density_low(k).wait_recv()

        scale = []
        for offset in range(5):
            z = slab * nz + p + offset - HALO
            scale.append(kernel_taps[offset] * per_distance(jnp.minimum(z, total_nz - 1 - z)))
        part = None
        for k in range(own):
            value = scale[0] * dens[k, p]
            for offset in range(1, 5):
                value = value + scale[offset] * dens[k, p + offset]
            spread = in_plane(value * inverse[...])
            marg[k, p] = spread
            term = weighted(k, spread)
            part = term if part is None else part + term
        return part

    def send_face(buf, send, recv, p):
        @pl.when(jnp.logical_and(has_low, p < HALO))
        def _():
            for k in range(own):
                plane_low(buf, send, recv, k, p).start()

        @pl.when(jnp.logical_and(has_high, p >= nz - HALO))
        def _():
            for k in range(own):
                plane_high(buf, send, recv, k, p).start()

    def wait_faces(buf, send, recv):
        @pl.when(has_low)
        def _():
            for k in range(own):
                for p in range(nz - HALO, nz):
                    plane_high(buf, send, recv, k, p).wait_recv()

        @pl.when(has_high)
        def _():
            for k in range(own):
                for p in range(HALO):
                    plane_low(buf, send, recv, k, p).wait_recv()

    def wait_sent(buf, send, recv):
        @pl.when(has_low)
        def _():
            for k in range(own):
                for p in range(HALO):
                    plane_low(buf, send, recv, k, p).wait_send()

        @pl.when(has_high)
        def _():
            for k in range(own):
                for p in range(nz - HALO, nz):
                    plane_high(buf, send, recv, k, p).wait_send()

    def first_use(g):
        p, c = order_first(g // CHUNKS), g % CHUNKS
        at = pl.ds(pl.multiple_of(c * rows, rows), rows)
        center = jnp.exp(inner[0, g])
        for k in range(own):
            scal[k, p + HALO, at] = center / marg[k, p, at]
        pl.when(c == CHUNKS - 1)(lambda: send_face(scal, s_send, s_recv, p))

    all_reduce(0, order_first, first_compute, first_use)

    wait_faces(scal, s_send, s_recv)

    def quotient(i, _):
        p = order_faces(i)
        for k in range(own):
            quot[k, p + HALO] = dens[k, p + HALO] / in_plane(along_z(scal, k, p))
        send_face(quot, q_send, q_recv, p)
        return 0

    lax.fori_loop(0, nz, quotient, 0)

    def second_compute(i, p):
        pl.when(i == nz - 4)(lambda: wait_faces(quot, q_send, q_recv))
        part = None
        for k in range(own):
            marginal = scal[k, p + HALO] * in_plane(along_z(quot, k, p))
            marg[k, p] = marginal
            term = weighted(k, marginal)
            part = term if part is None else part + term
        return part

    def center_store(p):
        return pltpu.make_async_copy(cent.at[p], center_out.at[p], out_sem.at[own, p])

    def scaling_store(k, p):
        return pltpu.make_async_copy(marg.at[k, p], scaling_out.at[k, p], out_sem.at[k, p])

    def second_use(g):
        p, c = order_second(g // CHUNKS), g % CHUNKS
        at = pl.ds(pl.multiple_of(c * rows, rows), rows)
        center = jnp.exp(inner[1, g])
        cent[p, at] = center
        for k in range(own):
            marg[k, p, at] = scal[k, p + HALO, at] * center / marg[k, p, at]

        @pl.when(c == CHUNKS - 1)
        def _():
            center_store(p).start()
            for k in range(own):
                scaling_store(k, p).start()

    all_reduce(1, order_second, second_compute, second_use)

    @pl.when(has_low)
    def _():
        for k in range(own):
            density_low(k).wait_send()

    @pl.when(has_high)
    def _():
        for k in range(own):
            density_high(k).wait_send()

    wait_sent(scal, s_send, s_recv)
    wait_sent(quot, q_send, q_recv)

    def drain(g, _):
        for t in range(ITERS):
            up_other(t, g).wait_send()
            pl.when(has_outer)(lambda: down_copy(t, g).wait_send())
        return 0

    lax.fori_loop(0, steps, drain, 0)

    def stored(p, _):
        center_store(p).wait()
        for k in range(own):
            scaling_store(k, p).wait()
        return 0

    lax.fori_loop(0, nz, stored, 0)


def per_device(slabs, vols, density, weights):
    own, nz, nx, ny = density.shape
    steps, rows = nz * CHUNKS, nx // CHUNKS
    padded = pltpu.VMEM((own, nz + 2 * HALO, nx, ny), jnp.float32)
    chunks = pltpu.VMEM((ITERS, steps, rows, ny), jnp.float32)
    dma = pltpu.SemaphoreType.DMA
    return pl.pallas_call(
        functools.partial(kernel, slabs, vols),
        out_shape=(
            jax.ShapeDtypeStruct((nz, nx, ny), jnp.float32),
            jax.ShapeDtypeStruct(density.shape, jnp.float32),
        ),
        in_specs=[pl.BlockSpec(memory_space=pltpu.SMEM), pl.BlockSpec(memory_space=pl.ANY)],
        out_specs=(pl.BlockSpec(memory_space=pl.ANY), pl.BlockSpec(memory_space=pl.ANY)),
        scratch_shapes=[
            padded, padded, padded,
            pltpu.VMEM((own, nz, nx, ny), jnp.float32),
            pltpu.VMEM((nz, nx, ny), jnp.float32),
            chunks, chunks, chunks,
            pltpu.VMEM((nx, ny), jnp.float32),
            pltpu.VMEM((nx, nx), jnp.float32),
            pltpu.VMEM((ny, ny), jnp.float32),
            dma((own,)), dma((own + 1, nz)),
            dma((2, own)), dma((2, own)),
            dma((2, own, HALO)), dma((2, own, HALO)),
            dma((2, own, HALO)), dma((2, own, HALO)),
            dma((ITERS, steps)), dma((ITERS, steps)),
            dma((ITERS, steps)), dma((ITERS, steps)),
        ],
        compiler_params=pltpu.CompilerParams(
            collective_id=0, has_side_effects=True, vmem_limit_bytes=52 * 1024 * 1024
        ),
    )(weights, density)


def solution(mesh):
    in_specs = (P(("groups", "vol"), "slab", None, None), P("groups"))
    out_specs = (P(("groups", "slab"), None, None), P(("groups", "vol"), "slab", None, None))
    body = functools.partial(per_device, mesh.shape["slab"], mesh.shape["vol"])
    return jax.shard_map(
        body, mesh=mesh, in_specs=in_specs, out_specs=out_specs, check_vma=False
    )
```

time: 342 us -> 148 us (0.43)
  waiting for transfers between devices: 208 us -> 0 us
  Pallas kernels: 0 us -> 142 us
  other arithmetic: 71.3 us -> 0 us
  starting transfers between devices: 38.3 us -> 0 us
  between operations: 14.3 us -> 0.66 us
    psum x2 -> x0, waiting for transfers between devices: 195 us -> none  [per_device(): log_mean = lax.psum(partial_value, 'vol')]
    pallas_call x0 -> x1, Pallas kernels: none -> 142 us  [per_device(): pl.pallas_call(functools.partial(kernel, slabs, vols), out_shape=(jax.Sha...]
    ppermute x8 -> x0, starting transfers between devices: 38.3 us -> none  [the longest x4 32.9 us: with_halo(): lax.ppermute(lax.slice_in_dim(block, block.shape[dim] - width, None, axis...]
    add x8 -> x0, other arithmetic: 32.2 us -> none  [blur_valid(): total + kernel_taps[offset] * lax.slice_in_dim(volume, offset, offset + l...]
    div x5 -> x0, other arithmetic: 23.6 us -> none  [the longest x2 17 us: per_device(): quotient = density / heat_padded(padded)]
    reduce_sum x3 -> x0, other arithmetic: 15.5 us -> none  [the longest x2 14.8 us: per_device(): jnp.sum(own_weights[:, None, None, None] * jnp.log(marginal), axis=0)]
    ppermute x8 -> x0, waiting for transfers between devices: 13.5 us -> none  [the longest x4 9.82 us: with_halo(): lax.ppermute(lax.slice_in_dim(block, 0, width, axis=dim), axis, backward)]
    exp x2 -> x0, local copies, waits for them, and re-layouts: 4.03 us -> none  [per_device(): center = jnp.exp(log_mean)]
  transfers between devices with their start and end apart: 10 -> 0, of which waited for: 9 -> 0; matrix products, arithmetic and copies ran while one was open for 0% -> 0% of each run, Pallas kernels for 0% -> 0%
where the time goes in v1:
time: 148 us
  Pallas kernels  142 us (96%)
  local copies, waits for them, and re-layouts  5.87 us (4%)
    pallas_call x1, Pallas kernels, per_device(): pl.pallas_call(functools.partial(kernel, slabs, vols), out_shape=(jax.Sha...  142 us
    unnamed x6, local copies, waits for them, and re-layouts  5.87 us

profile of v1, /device:TPU:0, one launch (start us, length us, event | category | flops | bytes accessed | tf_op | source)
XLA Modules:
  0.0 148.3 jit_solution(8005149677260785318)
XLA Ops:
  0.6 0.0 copy-start
  0.6 0.6 copy-done
  1.3 141.8 %shard_map.41 = (f32[8,256,256]{2,1,0:T(8,128)}, f32[2,8,256,256]{3,2,1,0:T(8,128)}) custom-call(f32[8]{0:T(128)S(1)} %copy-done, f32[2,8,256,256]{3,2,1,0:T(8,128)} %density.1), custom_call_target="tpu_custom_call" | custom-call | tf_op jit(solution)/shard_map/pallas_call | solution.py:388
  143.1 0.0 copy-start.1
  143.1 3.2 %copy.6 = f32[8,256,256]{2,1,0:T(8,128)} copy(f32[8,256,256]{2,1,0:T(8,128)} %get-tuple-element.4) | data formatting | bytes 4194304
  146.3 0.0 copy-done.1
  146.3 2.0 %copy.7 = f32[2,8,256,256]{3,2,1,0:T(8,128)} copy(f32[2,8,256,256]{3,2,1,0:T(8,128)S(1)} %copy-done.1) | data formatting | bytes 8388608
Async XLA Ops:
  0.6 0.7 copy-start
  143.1 3.2 %copy-start.1 = (f32[2,8,256,256]{3,2,1,0:T(8,128)S(1)}, f32[2,8,256,256]{3,2,1,0:T(8,128)}, u32[]{:S(2)}) copy-start(f32[2,8,256,256]{3,2,1,0:T(8,128)} %get-tuple-element.5) | copy-start | bytes 12582916

commit v2 on v1

--- a/solution.py
+++ b/solution.py
@@ -48,8 +48,9 @@
     outward = jnp.where(low_side, vol - 1, vol + 1)
     depth = jnp.where(low_side, half - 1 - vol, vol - half)
     is_center = depth == 0
+    early = depth > 0
     has_outer = depth < half - 1
-    lag = 2 + 5 * depth
+    lag = jnp.minimum(4 + 10 * depth, steps)
     has_low, has_high = slab > 0, slab < slabs - 1
 
     barrier = pltpu.get_barrier_semaphore()
@@ -123,8 +124,11 @@
         for buf in (dens, scal, quot):
             buf[:, nz + HALO :] = jnp.zeros((own, HALO, nx, ny), jnp.float32)
 
-    band_x[...] = band(nx)
-    band_y[...] = band(ny)
+    for taps, size in ((band_x, nx), (band_y, ny)):
+        whole = band(size)
+        high = whole.astype(jnp.bfloat16)
+        taps[0] = high
+        taps[1] = (whole - high.astype(jnp.float32)).astype(jnp.bfloat16)
     at_x = lax.broadcasted_iota(jnp.int32, (nx, ny), 0)
     at_y = lax.broadcasted_iota(jnp.int32, (nx, ny), 1)
     inverse[...] = per_distance(jnp.minimum(at_x, nx - 1 - at_x)) * per_distance(
@@ -141,11 +145,18 @@
         for k in range(own)
     ]
 
+    def split(value):
+        high = value.astype(jnp.bfloat16)
+        return high, (value - high.astype(jnp.float32)).astype(jnp.bfloat16)
+
+    def dot(a, b):
+        return jnp.dot(a, b, preferred_element_type=jnp.float32)
+
     def in_plane(value):
-        dot = functools.partial(
-            jnp.dot, precision=lax.Precision.HIGHEST, preferred_element_type=jnp.float32
-        )
-        return dot(band_x[...], dot(value, band_y[...]))
+        high, low = split(value)
+        blurred = dot(high, band_y[0]) + (dot(high, band_y[1]) + dot(low, band_y[0]))
+        high, low = split(blurred)
+        return dot(band_x[0], high) + (dot(band_x[1], high) + dot(band_x[0], low))
 
     def along_z(buf, k, p):
         total = kernel_taps[0] * (buf[k, p] + buf[k, p + 4])
@@ -158,10 +169,6 @@
     def order_first(i):
         late, last = (i + nz - 2) // nz, (i + nz - 6) // nz
         return (1 - late) * (i + 2) + (late - last) * faces(jnp.maximum(i - 2, 0)) + last * (i - 2)
-
-    def order_faces(i):
-        late = (i + nz - 4) // nz
-        return (1 - late) * faces(i) + late * (i - 2)
 
     def order_second(i):
         late = (i + 4) // nz
@@ -270,13 +277,14 @@
             for k in range(own):
                 plane_high(buf, send, recv, k, p).start()
 
-    def wait_faces(buf, send, recv):
+    def wait_low(buf, send, recv):
         @pl.when(has_low)
         def _():
             for k in range(own):
                 for p in range(nz - HALO, nz):
                     plane_high(buf, send, recv, k, p).wait_recv()
 
+    def wait_high(buf, send, recv):
         @pl.when(has_high)
         def _():
             for k in range(own):
@@ -296,29 +304,52 @@
                 for p in range(nz - HALO, nz):
                     plane_high(buf, send, recv, k, p).wait_send()
 
+    def quotient(p):
+        for k in range(own):
+            quot[k, p + HALO] = dens[k, p + HALO] / in_plane(along_z(scal, k, p))
+        send_face(quot, q_send, q_recv, p)
+
+    def quotients(start, stop):
+        def one(p, _):
+            quotient(p)
+            return 0
+
+        lax.fori_loop(start, stop, one, 0)
+
+    def quotients_low():
+        wait_low(scal, s_send, s_recv)
+        quotients(0, HALO)
+
     def first_use(g):
-        p, c = order_first(g // CHUNKS), g % CHUNKS
+        i, c = g // CHUNKS, g % CHUNKS
+        p = order_first(i)
         at = pl.ds(pl.multiple_of(c * rows, rows), rows)
         center = jnp.exp(inner[0, g])
         for k in range(own):
             scal[k, p + HALO, at] = center / marg[k, p, at]
-        pl.when(c == CHUNKS - 1)(lambda: send_face(scal, s_send, s_recv, p))
+
+        @pl.when(c == CHUNKS - 1)
+        def _():
+            send_face(scal, s_send, s_recv, p)
+            pl.when(jnp.logical_and(i == nz - 2, early))(quotients_low)
 
     all_reduce(0, order_first, first_compute, first_use)
 
-    wait_faces(scal, s_send, s_recv)
-
-    def quotient(i, _):
-        p = order_faces(i)
-        for k in range(own):
-            quot[k, p + HALO] = dens[k, p + HALO] / in_plane(along_z(scal, k, p))
-        send_face(quot, q_send, q_recv, p)
-        return 0
-
-    lax.fori_loop(0, nz, quotient, 0)
+    pl.when(jnp.logical_not(early))(quotients_low)
+    quotients(HALO, HALO + 3)
+    wait_high(scal, s_send, s_recv)
+    quotients(nz - 1, nz)
 
     def second_compute(i, p):
-        pl.when(i == nz - 4)(lambda: wait_faces(quot, q_send, q_recv))
+        @pl.when(jnp.logical_and(i >= 1, i < nz - 5))
+        def _():
+            quotient(i + 4)
+
+        @pl.when(i == nz - 4)
+        def _():
+            wait_low(quot, q_send, q_recv)
+            wait_high(quot, q_send, q_recv)
+
         part = None
         for k in range(own):
             marginal = scal[k, p + HALO] * in_plane(along_z(quot, k, p))
@@ -399,8 +430,8 @@
             pltpu.VMEM((nz, nx, ny), jnp.float32),
             chunks, chunks, chunks,
             pltpu.VMEM((nx, ny), jnp.float32),
-            pltpu.VMEM((nx, nx), jnp.float32),
-            pltpu.VMEM((ny, ny), jnp.float32),
+            pltpu.VMEM((2, nx, nx), jnp.bfloat16),
+            pltpu.VMEM((2, ny, ny), jnp.bfloat16),
             dma((own,)), dma((own + 1, nz)),
             dma((2, own)), dma((2, own)),
             dma((2, own, HALO)), dma((2, own, HALO)),

time: 148 us -> 133 us (0.90)
  Pallas kernels: 142 us -> 127 us
    pallas_call x1, Pallas kernels: 142 us -> 127 us  [per_device(): pl.pallas_call(functools.partial(kernel, slabs, vols), out_shape=(jax.Sha...]
where the time goes in v2:
time: 133 us
  Pallas kernels  127 us (95%)
  local copies, waits for them, and re-layouts  5.87 us (4%)
    pallas_call x1, Pallas kernels, per_device(): pl.pallas_call(functools.partial(kernel, slabs, vols), out_shape=(jax.Sha...  127 us
    unnamed x6, local copies, waits for them, and re-layouts  5.87 us

profile of v2, /device:TPU:0, one launch (start us, length us, event | category | flops | bytes accessed | tf_op | source)
XLA Modules:
  0.0 133.2 jit_solution(7226675857663626403)
XLA Ops:
  0.6 0.0 copy-start
  0.6 0.6 copy-done
  1.3 126.7 %shard_map.41 = (f32[8,256,256]{2,1,0:T(8,128)}, f32[2,8,256,256]{3,2,1,0:T(8,128)}) custom-call(f32[8]{0:T(128)S(1)} %copy-done, f32[2,8,256,256]{3,2,1,0:T(8,128)} %density.1), custom_call_target="tpu_custom_call" | custom-call | tf_op jit(solution)/shard_map/pallas_call | solution.py:419
  127.9 0.0 copy-start.1
  128.0 3.2 %copy.6 = f32[8,256,256]{2,1,0:T(8,128)} copy(f32[8,256,256]{2,1,0:T(8,128)} %get-tuple-element.4) | data formatting | bytes 4194304
  131.2 0.0 copy-done.1
  131.2 2.0 %copy.7 = f32[2,8,256,256]{3,2,1,0:T(8,128)} copy(f32[2,8,256,256]{3,2,1,0:T(8,128)S(1)} %copy-done.1) | data formatting | bytes 8388608
Async XLA Ops:
  0.6 0.7 copy-start
  127.9 3.2 %copy-start.1 = (f32[2,8,256,256]{3,2,1,0:T(8,128)S(1)}, f32[2,8,256,256]{3,2,1,0:T(8,128)}, u32[]{:S(2)}) copy-start(f32[2,8,256,256]{3,2,1,0:T(8,128)} %get-tuple-element.5) | copy-start | bytes 12582916

commit v3 on v2

--- a/solution.py
+++ b/solution.py
@@ -76,16 +76,16 @@
             device_id=device, device_id_type=pl.DeviceIdType.MESH,
         )
 
-    def density_low(k):
-        return remote(
-            density.at[k, pl.ds(0, HALO)], dens.at[k, pl.ds(nz + HALO, HALO)],
-            d_send.at[0, k], d_recv.at[0, k], {"slab": slab - 1},
-        )
-
-    def density_high(k):
-        return remote(
-            density.at[k, pl.ds(nz - HALO, HALO)], dens.at[k, pl.ds(0, HALO)],
-            d_send.at[1, k], d_recv.at[1, k], {"slab": slab + 1},
+    def density_low(k, near):
+        return remote(
+            density.at[k, near], dens.at[k, nz + HALO + near],
+            d_send.at[0, k, near], d_recv.at[0, k, near], {"slab": slab - 1},
+        )
+
+    def density_high(k, near):
+        return remote(
+            density.at[k, nz - 1 - near], dens.at[k, HALO - 1 - near],
+            d_send.at[1, k, near], d_recv.at[1, k, near], {"slab": slab + 1},
         )
 
     def plane_low(buf, send, recv, k, p):
@@ -106,13 +106,15 @@
 
     @pl.when(has_low)
     def _():
-        for k in range(own):
-            density_low(k).start()
+        for near in range(HALO):
+            for k in range(own):
+                density_low(k, near).start()
 
     @pl.when(has_high)
     def _():
-        for k in range(own):
-            density_high(k).start()
+        for near in range(HALO):
+            for k in range(own):
+                density_high(k, near).start()
 
     @pl.when(jnp.logical_not(has_low))
     def _():
@@ -164,7 +166,8 @@
         return total + kernel_taps[2] * buf[k, p + 2]
 
     def faces(i):
-        return i // 2 + (i % 2) * (nz - 1 - 2 * (i // 2))
+        near = 1 - i // 2
+        return near + (i % 2) * (nz - 1 - 2 * near)
 
     def order_first(i):
         late, last = (i + nz - 2) // nz, (i + nz - 6) // nz
@@ -239,17 +242,16 @@
         load.wait()
 
     def first_compute(i, p):
-        @pl.when(i == 2)
-        def _():
-            @pl.when(has_low)
+        for near in range(HALO):
+            @pl.when(jnp.logical_and(i == 2 + 2 * near, has_low))
             def _():
                 for k in range(own):
-                    density_high(k).wait_recv()
-
-            @pl.when(has_high)
+                    density_high(k, near).wait_recv()
+
+            @pl.when(jnp.logical_and(i == 2 + 2 * near, has_high))
             def _():
                 for k in range(own):
-                    density_low(k).wait_recv()
+                    density_low(k, near).wait_recv()
 
         scale = []
         for offset in range(5):
@@ -382,13 +384,15 @@
 
     @pl.when(has_low)
     def _():
-        for k in range(own):
-            density_low(k).wait_send()
+        for near in range(HALO):
+            for k in range(own):
+                density_low(k, near).wait_send()
 
     @pl.when(has_high)
     def _():
-        for k in range(own):
-            density_high(k).wait_send()
+        for near in range(HALO):
+            for k in range(own):
+                density_high(k, near).wait_send()
 
     wait_sent(scal, s_send, s_recv)
     wait_sent(quot, q_send, q_recv)
@@ -433,7 +437,7 @@
             pltpu.VMEM((2, nx, nx), jnp.bfloat16),
             pltpu.VMEM((2, ny, ny), jnp.bfloat16),
             dma((own,)), dma((own + 1, nz)),
-            dma((2, own)), dma((2, own)),
+            dma((2, own, HALO)), dma((2, own, HALO)),
             dma((2, own, HALO)), dma((2, own, HALO)),
             dma((2, own, HALO)), dma((2, own, HALO)),
             dma((ITERS, steps)), dma((ITERS, steps)),

time: 133 us -> 131 us (0.985)
  Pallas kernels: 127 us -> 124 us
    pallas_call x1, Pallas kernels: 127 us -> 124 us  [per_device(): pl.pallas_call(functools.partial(kernel, slabs, vols), out_shape=(jax.Sha...]
where the time goes in v3:
time: 131 us
  Pallas kernels  124 us (95%)
  local copies, waits for them, and re-layouts  5.87 us (4%)
    pallas_call x1, Pallas kernels, per_device(): pl.pallas_call(functools.partial(kernel, slabs, vols), out_shape=(jax.Sha...  124 us
    unnamed x6, local copies, waits for them, and re-layouts  5.87 us

profile of v3, /device:TPU:0, one launch (start us, length us, event | category | flops | bytes accessed | tf_op | source)
XLA Modules:
  0.0 130.8 jit_solution(17032870499380184762)
XLA Ops:
  0.6 0.0 copy-start
  0.6 0.6 copy-done
  1.3 124.3 %shard_map.41 = (f32[8,256,256]{2,1,0:T(8,128)}, f32[2,8,256,256]{3,2,1,0:T(8,128)}) custom-call(f32[8]{0:T(128)S(1)} %copy-done, f32[2,8,256,256]{3,2,1,0:T(8,128)} %density.1), custom_call_target="tpu_custom_call" | custom-call | tf_op jit(solution)/shard_map/pallas_call | solution.py:423
  125.6 0.0 copy-start.1
  125.6 3.2 %copy.6 = f32[8,256,256]{2,1,0:T(8,128)} copy(f32[8,256,256]{2,1,0:T(8,128)} %get-tuple-element.4) | data formatting | bytes 4194304
  128.8 0.0 copy-done.1
  128.8 2.0 %copy.7 = f32[2,8,256,256]{3,2,1,0:T(8,128)} copy(f32[2,8,256,256]{3,2,1,0:T(8,128)S(1)} %copy-done.1) | data formatting | bytes 8388608
Async XLA Ops:
  0.6 0.7 copy-start
  125.6 3.2 %copy-start.1 = (f32[2,8,256,256]{3,2,1,0:T(8,128)S(1)}, f32[2,8,256,256]{3,2,1,0:T(8,128)}, u32[]{:S(2)}) copy-start(f32[2,8,256,256]{3,2,1,0:T(8,128)} %get-tuple-element.5) | copy-start | bytes 12582916

commit v4 on v3

--- a/solution.py
+++ b/solution.py
@@ -50,7 +50,7 @@
     is_center = depth == 0
     early = depth > 0
     has_outer = depth < half - 1
-    lag = jnp.minimum(4 + 10 * depth, steps)
+    lag = jnp.minimum(3 + 9 * depth, steps)
     has_low, has_high = slab > 0, slab < slabs - 1
 
     barrier = pltpu.get_barrier_semaphore()

time: 131 us -> 130 us (level)
  no operation moved by 1% of the time
where the time goes in v4:
time: 130 us
  Pallas kernels  123 us (95%)
  local copies, waits for them, and re-layouts  5.87 us (5%)
    pallas_call x1, Pallas kernels, per_device(): pl.pallas_call(functools.partial(kernel, slabs, vols), out_shape=(jax.Sha...  123 us
    unnamed x6, local copies, waits for them, and re-layouts  5.87 us

profile of v4, /device:TPU:0, one launch (start us, length us, event | category | flops | bytes accessed | tf_op | source)
XLA Modules:
  0.0 129.5 jit_solution(4606190567181392783)
XLA Ops:
  0.6 0.0 copy-start
  0.6 0.6 copy-done
  1.3 123.0 %shard_map.41 = (f32[8,256,256]{2,1,0:T(8,128)}, f32[2,8,256,256]{3,2,1,0:T(8,128)}) custom-call(f32[8]{0:T(128)S(1)} %copy-done, f32[2,8,256,256]{3,2,1,0:T(8,128)} %density.1), custom_call_target="tpu_custom_call" | custom-call | tf_op jit(solution)/shard_map/pallas_call | solution.py:423
  124.3 0.0 copy-start.1
  124.3 3.2 %copy.6 = f32[8,256,256]{2,1,0:T(8,128)} copy(f32[8,256,256]{2,1,0:T(8,128)} %get-tuple-element.4) | data formatting | bytes 4194304
  127.5 0.0 copy-done.1
  127.5 2.0 %copy.7 = f32[2,8,256,256]{3,2,1,0:T(8,128)} copy(f32[2,8,256,256]{3,2,1,0:T(8,128)S(1)} %copy-done.1) | data formatting | bytes 8388608
Async XLA Ops:
  0.6 0.7 copy-start
  124.3 3.2 %copy-start.1 = (f32[2,8,256,256]{3,2,1,0:T(8,128)S(1)}, f32[2,8,256,256]{3,2,1,0:T(8,128)}, u32[]{:S(2)}) copy-start(f32[2,8,256,256]{3,2,1,0:T(8,128)} %get-tuple-element.5) | copy-start | bytes 12582916
